TPU v7x, 256 devices: a whole 4x4x8 slice. The times are simulated.
256 devices in a mesh: seq: 16 (over x_lo, y, core), head: 8 (over z), batch: 2 (over x_hi).
Axes of the slice: x: 4 (x_hi: 2, x_lo: 2; x = x_hi * 2 + x_lo), y: 4, z: 8, core: 2. Of those that a mesh axis runs over, the one named last changes fastest.
Arguments:
- query_vectors: bfloat16 [4, 16384, 2048], P('batch', 'seq', 'head'), parts along dimension 0, may hold values from -6 to 6
- key_vectors: bfloat16 [4, 16384, 2048], P('batch', 'seq', 'head'), parts along dimension 0, may hold values from -6 to 6
- value_vectors: bfloat16 [4, 16384, 2048], P('batch', 'seq', 'head'), parts along dimension 0, may hold values from -6 to 6
- token_rates: float32 [4, 16, 16384], P('batch', 'head', 'seq'), parts along dimension 0, may hold values from 0.05 to 1
- gate_weight: float32 [16, 128, 256], P('head'), may hold values from -0.5 to 0.5
- up_weight: float32 [16, 128, 256], P('head'), may hold values from -0.5 to 0.5
- down_weight: float32 [16, 128, 256], P('head'), may hold values from -0.375 to 0.375
- step_sizes: float32 [16], P('head'), may hold values from 0.3 to 1
- norm_gain: float32 [2048], P('head'), may hold values from 0.1 to 1.9
Outputs:
- mixed: bfloat16 [4, 16384, 2048], P('batch', 'seq', 'head'), parts along dimension 0
- final_weights: float32 [6, 16, 128, 256], P('batch', 'head'), parts along dimension 0
There are 2 independent parts, one for each index of `batch`. A program takes and returns all parts, laid end to end along the dimension named above; an argument that names none is the same for every part. Nothing has to cross between parts.
All inputs are finite; a program needn't handle non-finite values.
Results may differ from a plain program's by a relative error of at most 0.008.
Values may be sent and summed in bfloat16 or wider, within the bound.
No kernel may reach another device: no remote copies, remote signals or barrier semaphores. Data moves between devices by JAX's collectives and lax.ppermute only.
A program may use at most 128 MiB of HBM per device.

v0:
```python
import functools
import math

import jax
import jax.numpy as jnp
from jax import lax
from jax.experimental import pallas as pl
from jax.experimental.pallas import tpu as pltpu
from jax.sharding import PartitionSpec as P

HD = 128
FW = 256
NS_STEPS = 5
ROWS = 256
SLOW_ROWS = 128
SLOW_MIX = 64

coeff_first = 3.4445
coeff_second = -4.775
coeff_third = 2.0315
frob_epsilon = 1e-07
rms_epsilon = 1e-06
column_epsilon = 1e-06

f32 = jnp.float32
bf16 = jnp.bfloat16
LEAST_SUM = 1e-25
MOST_SUM = 1e30
NO_KEYS = -1e30
VMEM_LIMIT = 62 * 1024 * 1024
SMALL_LIMIT = 24 * 1024 * 1024
STEP_LIMIT = 24 * 1024 * 1024
PART_LIMIT = 32 * 1024 * 1024


def dot(a, b, over=((1,), (0,))):
    return lax.dot_general(a, b, (over, ((), ())), preferred_element_type=f32)


def sigmoid(x):
    return 0.5 * jnp.tanh(0.5 * x) + 0.5


def move(block, route):
    return lax.ppermute(block, "seq", [(i, route(i)) for i in range(lax.axis_size("seq"))])


def fetch(copies, sems, at=0):
    started = [pltpu.make_async_copy(a, b, sems.at[at + i]) for i, (a, b) in enumerate(copies)]
    for copy in started:
        copy.start()
    return started


def fetch(copies, sems, at=0):
    started = [pltpu.make_async_copy(a, b, sems.at[at + i]) for i, (a, b) in enumerate(copies)]
    for copy in started:
        copy.start()
    return started


def grads_kernel(group, k_ref, v_ref, r_ref, *refs):
    if k_ref.ndim == 3:
        k_ref, v_ref, r_ref = k_ref.at[group], v_ref.at[group], r_ref.at[group]
    *w_refs, out_ref, grad_ref, hid_ref, og_ref = refs
    if len(w_refs) > 1:
        step_ref, *w_refs, kept_ref, limits_ref = w_refs
        for which in range(3):
            weight = w_refs[which][...]
            kept_ref[which] = weight
            limits_ref[which, :, :1] = jnp.sqrt(jnp.sum(weight * weight, axis=1, keepdims=True))
            for h in range(weight.shape[0]):
                limits_ref[which, h, 1:] = jnp.full((1, FW), step_ref[h], f32)
    else:
        w_refs = [w_refs[0].at[which] for which in range(3)]
    tokens, width = k_ref.shape
    for h in range(width // HD):
        lanes = slice(h * HD, (h + 1) * HD)
        low_gate, low_up, low_down = (w_ref[h].astype(bf16) for w_ref in w_refs)
        for c in range(tokens // ROWS):
            rows = slice(c * ROWS, (c + 1) * ROWS)
            keys = k_ref[rows, lanes]
            rate = jnp.broadcast_to(r_ref[h : h + 1, rows], (HD, ROWS)).T
            out_grad = (-rate * v_ref[rows, lanes].astype(f32)).astype(bf16)
            gate_pre = dot(keys, low_gate)
            up_pre = dot(keys, low_up)
            hidden_grad = dot(out_grad, low_down)
            sig = sigmoid(gate_pre)
            active = gate_pre * sig
            og_ref[rows] = out_grad
            hid_ref[rows] = (active * up_pre).astype(bf16)
            grad_ref[rows, FW:] = (hidden_grad * active).astype(bf16)
            grad_ref[rows, :FW] = (
                hidden_grad * up_pre * sig * (1.0 + gate_pre * (1.0 - sig))
            ).astype(bf16)
        both = dot(k_ref[:, lanes], grad_ref[...], ((0,), (0,)))
        down = dot(og_ref[...], hid_ref[...], ((0,), (0,)))
        for which, full in enumerate((both[:, :FW], both[:, FW:], down)):
            for half in range(2):
                out_ref[which, h, half] = full[:, half * HD : (half + 1) * HD].astype(bf16)


def local_grads(group, keys, values, rates, weights, step_sizes=None):
    _, tokens, width = keys.shape
    heads = width // HD
    vmem = pl.BlockSpec(memory_space=pltpu.VMEM)
    out_shape = [jax.ShapeDtypeStruct((3, heads, 2, HD, HD), bf16)]
    if step_sizes is None:
        extra, limit = [], SMALL_LIMIT
        in_specs = [vmem] * (3 + len(weights))
        out_specs = [vmem]
    else:
        extra, limit = [step_sizes], VMEM_LIMIT
        group_rows = pl.BlockSpec((None, tokens, width), lambda i: (group, 0, 0))
        in_specs = (
            [group_rows] * 2
            + [pl.BlockSpec((None, heads, tokens), lambda i: (group, 0, 0))]
            + [pl.BlockSpec(memory_space=pltpu.SMEM)]
            + [pl.BlockSpec((heads, HD, FW), lambda i: (0, 0, 0))] * len(weights)
        )
        out_shape = [
            jax.ShapeDtypeStruct((3, heads, HD, FW), f32),
            jax.ShapeDtypeStruct((3, heads, 2, FW), f32),
        ] + out_shape
        out_specs = [pl.BlockSpec(o.shape, lambda i, n=len(o.shape): (0,) * n) for o in out_shape]
    return pl.pallas_call(
        functools.partial(grads_kernel, group),
        out_shape=out_shape,
        grid=(1,) if extra else (),
        in_specs=in_specs,
        out_specs=out_specs,
        scratch_shapes=[
            pltpu.VMEM((tokens, 2 * FW), bf16),
            pltpu.VMEM((tokens, FW), bf16),
            pltpu.VMEM((tokens, HD), bf16),
        ],
        compiler_params=pltpu.CompilerParams(vmem_limit_bytes=limit),
        cost_estimate=pl.CostEstimate(
            flops=12 * heads * tokens * HD * FW,
            bytes_accessed=4 * tokens * width,
            transcendentals=heads * tokens * FW,
        ),
        name="local_grads",
    )(keys, values, rates, *extra, *weights)


def split(x):
    high = x.astype(bf16)
    return high, (x - high.astype(f32)).astype(bf16)


def sweeps(x_ref, count):
    def sweep(_, carry):
        pieces, grams, polynomials = [], [], []
        for m in range(count):
            high, low = split(x_ref[m])
            pieces.append((high, low))
            stacked = jnp.concatenate([high, low], axis=0)
            g = dot(stacked, stacked, ((1,), (1,)))
            grams.append(g[:HD, :HD] + (g[HD:, :HD] + g[:HD, HD:]) + g[HD:, HD:])
        for m in range(count):
            row = jnp.concatenate(split(grams[m]), axis=1)
            squared = dot(row, jnp.concatenate([row, row], axis=0))
            polynomials.append(
                coeff_second * grams[m] + coeff_third * (squared[:, :HD] + squared[:, HD:])
            )
        for m in range(count):
            high, low = pieces[m]
            row = jnp.concatenate(split(polynomials[m]), axis=1)
            product = dot(row, jnp.concatenate([high, high], axis=0)) + dot(
                row, jnp.concatenate([low, low], axis=0)
            )
            x_ref[m] = coeff_first * x_ref[m] + product
        return carry

    lax.fori_loop(0, NS_STEPS, sweep, 0)


def step_kernel(s_ref, w_hbm, limits_hbm, out_hbm, x_ref, w_ref, limits_ref, out_ref, sems):
    heads = out_ref.shape[1]
    started = fetch([(w_hbm, w_ref), (limits_hbm, limits_ref)], sems)
    for which in range(3):
        for h in range(heads):
            grad = jnp.concatenate([s_ref[which, h, 0], s_ref[which, h, 1]], axis=1).astype(f32)
            frobenius = jnp.sqrt(jnp.sum(grad * grad, keepdims=True))
            x_ref[which * heads + h] = grad / (frobenius + frob_epsilon)
    sweeps(x_ref, 3 * heads)
    for copy in started:
        copy.wait()
    written = []
    for which in range(3):
        for h in range(heads):
            target = limits_ref[which, h, :1]
            stepped = w_ref[which, h] - limits_ref[which, h, 1:] * x_ref[which * heads + h]
            length = jnp.sqrt(jnp.sum(stepped * stepped, axis=0, keepdims=True))
            out_ref[which, h] = stepped * (target / (length + column_epsilon))
        copy = pltpu.make_async_copy(out_ref.at[which], out_hbm.at[which], sems.at[2 + which])
        copy.start()
        written.append(copy)
    for copy in written:
        copy.wait()


def step(summed, weights, limits):
    heads = weights.shape[1]
    everywhere = pl.BlockSpec(memory_space=pl.ANY)
    return pl.pallas_call(
        step_kernel,
        out_shape=jax.ShapeDtypeStruct(weights.shape, f32),
        in_specs=[pl.BlockSpec(memory_space=pltpu.VMEM), everywhere, everywhere],
        out_specs=everywhere,
        scratch_shapes=[
            pltpu.VMEM((3 * heads, HD, FW), f32),
            pltpu.VMEM(weights.shape, f32),
            pltpu.VMEM(limits.shape, f32),
            pltpu.VMEM(weights.shape, f32),
            pltpu.SemaphoreType.DMA((5,)),
        ],
        compiler_params=pltpu.CompilerParams(vmem_limit_bytes=STEP_LIMIT),
        cost_estimate=pl.CostEstimate(
            flops=3 * heads * NS_STEPS * 40 * HD * HD * FW,
            bytes_accessed=3 * heads * 10 * HD * FW,
            transcendentals=0,
        ),
        name="weight_step",
    )(summed, weights, limits)


def mix_kernel(group, rank_ref, *refs):
    (
        q_hbm, k_hbm, v_hbm, ks_hbm, vs_hbm, kf_hbm, vf_hbm, kb_hbm, vb_hbm, w_hbm, gain_hbm,
        out_hbm, q_ref, ko_ref, vo_ref, kf_ref, vf_ref, kn_ref, vn_ref, w_ref, gain_ref,
        normed_ref, out_ref, sems,
    ) = refs
    tokens, width = q_ref.shape
    heads = width // HD
    scale = 1.0 / math.sqrt(HD)
    power = scale * math.log2(math.e)
    blocks = tokens // ROWS
    odd = rank_ref[0] % 2 == 1
    started = fetch(
        [
            (w_hbm, w_ref),
            (gain_hbm, gain_ref),
            (q_hbm.at[group], q_ref),
            (k_hbm.at[group], ko_ref),
            (v_hbm.at[group], vo_ref),
            (kf_hbm, kf_ref),
            (vf_hbm, vf_ref),
        ],
        sems,
    )
    beside = [(ks_hbm.at[group], kn_ref), (vs_hbm.at[group], vn_ref)]
    behind = [(kb_hbm, kn_ref), (vb_hbm, vn_ref)]

    @pl.when(odd)
    def _():
        fetch(beside, sems, 7)

    @pl.when(jnp.logical_not(odd))
    def _():
        fetch(behind, sems, 7)

    started += [pltpu.make_async_copy(a, b, sems.at[7 + i]) for i, (a, b) in enumerate(behind)]
    for copy in started[:3]:
        copy.wait()
    all_lanes = [slice(h * HD, (h + 1) * HD) for h in range(heads)]
    all_rows = [slice(b * ROWS, (b + 1) * ROWS) for b in range(blocks)]
    for h, lanes in enumerate(all_lanes):
        low_gate, low_up, low_down = (w_ref[which, h].astype(bf16) for which in range(3))
        for rows in all_rows:
            q = q_ref[rows, lanes]
            gate_pre = dot(q, low_gate)
            hidden = (gate_pre * sigmoid(gate_pre) * dot(q, low_up)).astype(bf16)
            applied = dot(hidden, low_down, ((1,), (1,)))
            mean = jnp.mean(applied * applied, axis=1, keepdims=True)
            normed_ref[rows, lanes] = applied * lax.rsqrt(mean + rms_epsilon) * gain_ref[:, lanes]
    for copy in started[3:]:
        copy.wait()

    near_valid = rank_ref[0] >= 1 if group == 0 else True
    far_valid = rank_ref[0] >= 2 if group == 0 else True

    def beside_ones(v, valid=True):
        wide = jnp.concatenate([v, jnp.ones((v.shape[0], HD), bf16)], axis=1)
        return wide if valid is True else wide * jnp.where(valid, 1.0, 0.0).astype(bf16)

    causal = lax.broadcasted_iota(jnp.int32, (ROWS, ROWS), 0) >= lax.broadcasted_iota(
        jnp.int32, (ROWS, ROWS), 1
    )

    def raised(q, keys):
        return jnp.exp2(dot(q, keys, ((1,), (1,))) * power).astype(bf16)

    wrong = jnp.zeros((ROWS, HD), f32)
    for lanes in all_lanes:
        for b, rows in enumerate(all_rows):
            q = q_ref[rows, lanes]
            own = dot(q, ko_ref[rows, lanes], ((1,), (1,)))
            far = dot(q, kf_ref[rows, lanes], ((1,), (1,)))
            edge = jnp.exp2(jnp.where(causal, own, far) * power)
            total = dot(
                jnp.where(causal, edge, 0.0).astype(bf16), beside_ones(vo_ref[rows, lanes])
            )
            total += dot(
                jnp.where(causal, 0.0, edge).astype(bf16),
                beside_ones(vf_ref[rows, lanes], far_valid),
            )
            total += dot(raised(q, kn_ref[:, lanes]), beside_ones(vn_ref[:, lanes], near_valid))
            if b > 0:
                past = slice(0, b * ROWS)
                total += dot(raised(q, ko_ref[past, lanes]), beside_ones(vo_ref[past, lanes]))
            if b < blocks - 1:
                rest = slice((b + 1) * ROWS, tokens)
                total += dot(
                    raised(q, kf_ref[rest, lanes]), beside_ones(vf_ref[rest, lanes], far_valid)
                )
            sums = total[:, HD:]
            out_ref[rows, lanes] = (normed_ref[rows, lanes] + total[:, :HD] / sums).astype(bf16)
            fine = (sums > LEAST_SUM) & (sums < MOST_SUM)
            wrong = jnp.maximum(wrong, jnp.where(fine, 0.0, 1.0))

    @pl.when(jnp.max(wrong) > 0.0)
    def _():
        def one_block(step, carry):
            h, b = step % heads, step // heads
            one_head = [pl.ds(pl.multiple_of(h * HD, HD), HD)]
            rows = pl.ds(pl.multiple_of(b * SLOW_MIX, SLOW_MIX), SLOW_MIX)
            place, column = places(b * SLOW_MIX, (SLOW_MIX, tokens))
            limit = jnp.where(far_valid, tokens, -1)
            least = jnp.where(near_valid, 0, tokens)
            lowest = jnp.float32(-jnp.inf)
            for lanes in one_head:
                q = q_ref[rows, lanes]
                far = dot(q, kf_ref[:, lanes], ((1,), (1,))) * scale
                far = jnp.where((column > place) & (column < limit), far, lowest)
                near = dot(q, kn_ref[:, lanes], ((1,), (1,))) * scale
                near = jnp.where(column >= least, near, lowest)
                own = dot(q, ko_ref[:, lanes], ((1,), (1,))) * scale
                own = jnp.where(column <= place, own, lowest)
                parts = ((far, vf_ref), (near, vn_ref), (own, vo_ref))
                most = jnp.max(own, axis=1, keepdims=True)
                for scores, _ in parts[:2]:
                    most = jnp.maximum(most, jnp.max(scores, axis=1, keepdims=True))
                total = jnp.zeros((SLOW_MIX, HD), f32)
                sums = jnp.zeros((SLOW_MIX, 1), f32)
                for scores, v_ref in parts:
                    e = jnp.exp(scores - most)
                    sums += jnp.sum(e, axis=1, keepdims=True)
                    total += dot(e.astype(bf16), v_ref[:, lanes])
                out_ref[rows, lanes] = (normed_ref[rows, lanes] + total / sums).astype(bf16)
            return carry

        lax.fori_loop(0, heads * (tokens // SLOW_MIX), one_block, 0)

    done = pltpu.make_async_copy(out_ref, out_hbm.at[group], sems.at[9])
    done.start()
    done.wait()


def mix(group, rank, queries, keys, values, early, context, weights, gain):
    groups, tokens, width = queries.shape
    heads = width // HD
    everywhere = pl.BlockSpec(memory_space=pl.ANY)
    block = pltpu.VMEM((tokens, width), bf16)
    return pl.pallas_call(
        functools.partial(mix_kernel, group),
        out_shape=jax.ShapeDtypeStruct(queries.shape, bf16),
        in_specs=[pl.BlockSpec(memory_space=pltpu.SMEM)] + [everywhere] * 11,
        out_specs=everywhere,
        scratch_shapes=[block] * 7
        + [
            pltpu.VMEM(weights.shape, f32),
            pltpu.VMEM(gain.shape, f32),
            pltpu.VMEM((tokens, width), f32),
            block,
            pltpu.SemaphoreType.DMA((10,)),
        ],
        compiler_params=pltpu.CompilerParams(vmem_limit_bytes=VMEM_LIMIT),
        cost_estimate=pl.CostEstimate(
            flops=heads * tokens * 2 * tokens * 8 * HD,
            bytes_accessed=16 * tokens * width,
            transcendentals=heads * tokens * 2 * tokens,
        ),
        name="mix",
    )(rank, queries, keys, values, *early, *context, weights, gain)


def raise_to(q, keys):
    power = math.log2(math.e) / math.sqrt(HD)
    return jnp.exp2(dot(q, keys, ((1,), (1,))) * power)


def with_ones(v):
    return jnp.concatenate([v, jnp.ones((v.shape[0], HD), bf16)], axis=1)


def weighted(e, v):
    return dot(e.astype(bf16), with_ones(v))


def from_maximum(q, parts):
    scores = []
    most = jnp.full((q.shape[0], 1), NO_KEYS, f32)
    for keys, _, allowed in parts:
        s = dot(q, keys, ((1,), (1,))) / math.sqrt(HD)
        scores.append(s)
        most = jnp.maximum(
            most, jnp.max(jnp.where(allowed, s, NO_KEYS), axis=1, keepdims=True)
        )
    total = jnp.zeros((q.shape[0], HD), f32)
    sums = jnp.zeros((q.shape[0], 1), f32)
    for s, (_, values, allowed) in zip(scores, parts):
        e = jnp.where(allowed, jnp.exp(jnp.where(allowed, s, most) - most), 0.0)
        sums += jnp.sum(e, axis=1, keepdims=True)
        total += dot(e.astype(bf16), values)
    some = sums > 0.0
    safe = jnp.where(some, sums, 1.0)
    level = jnp.where(some, most + jnp.log(safe), NO_KEYS)
    return total / safe, jnp.broadcast_to(level, total.shape)


def unsafe(sums):
    return jnp.where((sums > LEAST_SUM) & (sums < MOST_SUM), 0.0, 1.0)


def places(first_row, shape):
    row = first_row + lax.broadcasted_iota(jnp.int32, shape, 0)
    return row, lax.broadcasted_iota(jnp.int32, shape, 1)


def remote_kernel(group, size, rank_ref, *refs):
    (
        q_hbm, k_hbm, v_hbm, ks_hbm, vs_hbm, out_ref, level_ref,
        q_ref, ko_ref, vo_ref, ks_ref, vs_ref, total_ref, sems,
    ) = refs
    tokens, width = q_ref.shape
    heads = width // HD
    blocks = tokens // ROWS
    rank = rank_ref[0]
    even = rank % 2 == 0
    at = jnp.where(rank >= size - 2, group - 1, group)
    started = fetch(
        [
            (q_hbm, q_ref),
            (k_hbm.at[at], ko_ref),
            (v_hbm.at[at], vo_ref),
            (ks_hbm.at[at], ks_ref),
            (vs_hbm.at[at], vs_ref),
        ],
        sems,
    )
    for copy in started[:3]:
        copy.wait()
    all_lanes = [slice(h * HD, (h + 1) * HD) for h in range(heads)]
    all_rows = [slice(b * ROWS, (b + 1) * ROWS) for b in range(blocks)]
    row, column = places(0, (ROWS, ROWS))
    for h, lanes in enumerate(all_lanes):
        for b, rows in enumerate(all_rows):
            q = q_ref[rows, lanes]
            e = jnp.where(column > row, raise_to(q, ko_ref[rows, lanes]), 0.0)
            total = weighted(e, vo_ref[rows, lanes])
            if b < blocks - 1:
                rest = slice((b + 1) * ROWS, tokens)
                total += weighted(raise_to(q, ko_ref[rest, lanes]), vo_ref[rest, lanes])
            total_ref[h, rows] = total
    for copy in started[3:]:
        copy.wait()

    @pl.when(even)
    def _():
        for h, lanes in enumerate(all_lanes):
            for rows in all_rows:
                e = raise_to(q_ref[rows, lanes], ks_ref[:, lanes])
                total_ref[h, rows] += weighted(e, vs_ref[:, lanes])

    wrong = jnp.zeros((ROWS, HD), f32)
    for h, lanes in enumerate(all_lanes):
        for b, rows in enumerate(all_rows):
            total = total_ref[h, rows]
            sums = total[:, HD:]
            some = sums > 0.0
            safe = jnp.where(some, sums, 1.0)
            out_ref[rows, lanes] = (total[:, :HD] / safe).astype(bf16)
            level = jnp.where(some, jnp.log(safe), NO_KEYS)
            level_ref[h, :, rows] = level.T[:8]
            bad = unsafe(sums)
            if b == blocks - 1:
                last = lax.broadcasted_iota(jnp.int32, bad.shape, 0) == ROWS - 1
                bad = jnp.where(last & jnp.logical_not(even), 0.0, bad)
            wrong = jnp.maximum(wrong, bad)

    @pl.when(jnp.max(wrong) > 0.0)
    def _():
        def one_block(step, carry):
            h, b = step % heads, step // heads
            one_head = [(h, pl.ds(pl.multiple_of(h * HD, HD), HD))]
            rows = pl.ds(pl.multiple_of(b * SLOW_ROWS, SLOW_ROWS), SLOW_ROWS)
            row, column = places(b * SLOW_ROWS, (SLOW_ROWS, tokens))
            everyone = column >= jnp.where(even, 0, tokens)
            for h, lanes in one_head:
                parts = (
                    (ko_ref[:, lanes], vo_ref[:, lanes], column > row),
                    (ks_ref[:, lanes], vs_ref[:, lanes], everyone),
                )
                values, level = from_maximum(q_ref[rows, lanes], parts)
                out_ref[rows, lanes] = values.astype(bf16)
                level_ref[h, :, rows] = level.T[:8]
            return carry

        lax.fori_loop(0, heads * (tokens // SLOW_ROWS), one_block, 0)


def remote_part(group, size, rank, received, keys, values, early):
    tokens, width = received.shape
    heads = width // HD
    everywhere = pl.BlockSpec(memory_space=pl.ANY)
    block = pltpu.VMEM((tokens, width), bf16)
    return pl.pallas_call(
        functools.partial(remote_kernel, group, size),
        out_shape=[
            jax.ShapeDtypeStruct((tokens, width), bf16),
            jax.ShapeDtypeStruct((heads, 8, tokens), f32),
        ],
        in_specs=[pl.BlockSpec(memory_space=pltpu.SMEM)] + [everywhere] * 5,
        out_specs=[pl.BlockSpec()] * 2,
        scratch_shapes=[block] * 5
        + [pltpu.VMEM((heads, tokens, 2 * HD), f32), pltpu.SemaphoreType.DMA((5,))],
        compiler_params=pltpu.CompilerParams(vmem_limit_bytes=PART_LIMIT),
        cost_estimate=pl.CostEstimate(
            flops=heads * tokens * tokens * 8 * HD,
            bytes_accessed=12 * tokens * width,
            transcendentals=heads * tokens * tokens,
        ),
        name="remote_part",
    )(rank, received, keys, values, *early)


def finish_kernel(group, _, rank_ref, *refs):
    (
        q_hbm, k_hbm, v_hbm, ks_hbm, vs_hbm, o_hbm, level_hbm, w_hbm, gain_hbm, out_hbm,
        q_ref, ko_ref, vo_ref, ks_ref, vs_ref, o_ref, level_ref, w_ref, gain_ref,
        normed_ref, total_ref, out_ref, sems,
    ) = refs
    tokens, width = q_ref.shape
    heads = width // HD
    blocks = tokens // ROWS
    odd = rank_ref[0] % 2 == 1
    started = fetch(
        [
            (w_hbm, w_ref),
            (gain_hbm, gain_ref),
            (q_hbm.at[group], q_ref),
            (k_hbm.at[group], ko_ref),
            (v_hbm.at[group], vo_ref),
            (ks_hbm.at[group], ks_ref),
            (vs_hbm.at[group], vs_ref),
            (o_hbm, o_ref),
            (level_hbm, level_ref),
        ],
        sems,
    )
    for copy in started[:3]:
        copy.wait()
    all_lanes = [slice(h * HD, (h + 1) * HD) for h in range(heads)]
    all_rows = [slice(b * ROWS, (b + 1) * ROWS) for b in range(blocks)]
    for h, lanes in enumerate(all_lanes):
        low_gate, low_up, low_down = (w_ref[which, h].astype(bf16) for which in range(3))
        for rows in all_rows:
            q = q_ref[rows, lanes]
            gate_pre = dot(q, low_gate)
            hidden = (gate_pre * sigmoid(gate_pre) * dot(q, low_up)).astype(bf16)
            applied = dot(hidden, low_down, ((1,), (1,)))
            mean = jnp.mean(applied * applied, axis=1, keepdims=True)
            normed_ref[rows, lanes] = applied * lax.rsqrt(mean + rms_epsilon) * gain_ref[:, lanes]
    for copy in started[3:]:
        copy.wait()
    row, column = places(0, (ROWS, ROWS))
    for h, lanes in enumerate(all_lanes):
        for b, rows in enumerate(all_rows):
            q = q_ref[rows, lanes]
            e = jnp.where(column <= row, raise_to(q, ko_ref[rows, lanes]), 0.0)
            total = weighted(e, vo_ref[rows, lanes])
            if b > 0:
                past = slice(0, b * ROWS)
                total += weighted(raise_to(q, ko_ref[past, lanes]), vo_ref[past, lanes])
            total_ref[h, rows] = total

    @pl.when(odd)
    def _():
        for h, lanes in enumerate(all_lanes):
            for rows in all_rows:
                e = raise_to(q_ref[rows, lanes], ks_ref[:, lanes])
                total_ref[h, rows] += weighted(e, vs_ref[:, lanes])

    def joined(rows, lanes, h, values, level):
        other = jnp.broadcast_to(level_ref[h, :1, rows], (HD, values.shape[0])).T
        share = sigmoid(other - level)
        attended = values + share * (o_ref[rows, lanes].astype(f32) - values)
        return (normed_ref[rows, lanes] + attended).astype(bf16)

    wrong = jnp.zeros((ROWS, HD), f32)
    for h, lanes in enumerate(all_lanes):
        for rows in all_rows:
            total = total_ref[h, rows]
            sums = total[:, HD:]
            out_ref[rows, lanes] = joined(rows, lanes, h, total[:, :HD] / sums, jnp.log(sums))
            wrong = jnp.maximum(wrong, unsafe(sums))

    @pl.when(jnp.max(wrong) > 0.0)
    def _():
        def one_block(step, carry):
            h, b = step % heads, step // heads
            one_head = [(h, pl.ds(pl.multiple_of(h * HD, HD), HD))]
            rows = pl.ds(pl.multiple_of(b * SLOW_ROWS, SLOW_ROWS), SLOW_ROWS)
            row, column = places(b * SLOW_ROWS, (SLOW_ROWS, tokens))
            everyone = column >= jnp.where(odd, 0, tokens)
            for h, lanes in one_head:
                parts = (
                    (ko_ref[:, lanes], vo_ref[:, lanes], column <= row),
                    (ks_ref[:, lanes], vs_ref[:, lanes], everyone),
                )
                values, level = from_maximum(q_ref[rows, lanes], parts)
                out_ref[rows, lanes] = joined(rows, lanes, h, values, level)
            return carry

        lax.fori_loop(0, heads * (tokens // SLOW_ROWS), one_block, 0)

    done = pltpu.make_async_copy(out_ref, out_hbm.at[group], sems.at[9])
    done.start()
    done.wait()


def finish(group, so_far, rank, queries, keys, values, early, far, weights, gain):
    groups, tokens, width = queries.shape
    heads = width // HD
    everywhere = pl.BlockSpec(memory_space=pl.ANY)
    block = pltpu.VMEM((tokens, width), bf16)
    return pl.pallas_call(
        functools.partial(finish_kernel, group),
        out_shape=jax.ShapeDtypeStruct(queries.shape, bf16),
        in_specs=[everywhere, pl.BlockSpec(memory_space=pltpu.SMEM)] + [everywhere] * 9,
        out_specs=everywhere,
        input_output_aliases={0: 0},
        scratch_shapes=[block] * 6
        + [
            pltpu.VMEM((heads, 8, tokens), f32),
            pltpu.VMEM(weights.shape, f32),
            pltpu.VMEM(gain.shape, f32),
            pltpu.VMEM((tokens, width), f32),
            pltpu.VMEM((heads, tokens, 2 * HD), f32),
            block,
            pltpu.SemaphoreType.DMA((10,)),
        ],
        compiler_params=pltpu.CompilerParams(vmem_limit_bytes=VMEM_LIMIT),
        cost_estimate=pl.CostEstimate(
            flops=heads * tokens * tokens * 14 * HD,
            bytes_accessed=16 * tokens * width,
            transcendentals=heads * tokens * 2 * tokens,
        ),
        name="finish",
    )(so_far, rank, queries, keys, values, *early, *far, weights, gain)


def add_kernel(x_ref, out_ref):
    total = jnp.sum(x_ref[...].astype(f32), axis=0).astype(bf16)
    for i in range(out_ref.shape[0]):
        out_ref[i] = total


def after(x, event):
    return lax.optimization_barrier((x, event))[0]


def exchange(tiles):
    return lax.all_to_all(tiles, "seq", 0, 0, tiled=True)


def add_parts(arrived):
    vmem = pl.BlockSpec(memory_space=pltpu.VMEM)
    return pl.pallas_call(
        add_kernel,
        out_shape=jax.ShapeDtypeStruct(arrived.shape, bf16),
        in_specs=[vmem],
        out_specs=vmem,
        compiler_params=pltpu.CompilerParams(vmem_limit_bytes=SMALL_LIMIT),
        name="add_parts",
    )(arrived)


def body(
    query_vectors,
    key_vectors,
    value_vectors,
    token_rates,
    gate_weight,
    up_weight,
    down_weight,
    step_sizes,
    norm_gain,
):
    rank = lax.axis_index("seq")
    size = lax.axis_size("seq")
    gain = norm_gain.reshape(1, -1)
    ranks = rank.astype(jnp.int32).reshape(1)

    def send(block, distance):
        return move(block, lambda i: (i + distance) % size)

    def swap(block):
        return move(block, lambda i: i ^ 1)

    together = lax.optimization_barrier
    first = (gate_weight, up_weight, down_weight)
    own = (query_vectors, key_vectors, value_vectors)
    far_keys = send(key_vectors[0], 2)
    weights, limits, partial = local_grads(
        0, key_vectors, value_vectors, token_rates, first, step_sizes
    )
    far_values = send(after(value_vectors[0], (far_keys, partial)), 2)
    asked = send(after(query_vectors[1], partial), -2)
    early = [swap(t) for t in own[1:]]
    added = add_parts(exchange(partial.reshape(size, -1, HD)))
    summed = exchange(added)
    answer = remote_part(1, size, ranks, after(asked, added), *own[1:], early)
    context = (far_keys, far_values, swap(far_keys), swap(far_values))
    summed, answer = together((summed, answer))
    far = [send(a, 2) for a in answer]
    later = step(summed.reshape(partial.shape), weights, limits)
    (partial,) = local_grads(1, key_vectors, value_vectors, token_rates, (later,))
    arrived = exchange(partial.reshape(size, -1, HD))
    mixed = mix(0, ranks, *own, early, context, weights, gain)
    arrived, mixed = together((arrived, mixed))
    summed = exchange(add_parts(arrived))
    mixed = finish(1, mixed, ranks, *own, early, far, later, gain)
    summed, mixed = together((summed, mixed))
    last = step(summed.reshape(partial.shape), later, limits)
    return mixed, last


def solution(mesh):
    return jax.shard_map(
        body,
        mesh=mesh,
        in_specs=(
            P("batch", "seq", "head"),
            P("batch", "seq", "head"),
            P("batch", "seq", "head"),
            P("batch", "head", "seq"),
            P("head", None, None),
            P("head", None, None),
            P("head", None, None),
            P("head"),
            P("head"),
        ),
        out_specs=(P("batch", "seq", "head"), P("batch", "head", None, None)),
        check_vma=False,
    )
```

profile of v0, /device:TPU:1, one launch (start us, length us, event | category | flops | bytes accessed | tf_op | source)
XLA Modules:
  0.0 143.0 jit_solution(17357214931894625192)
XLA Ops:
  0.6 3.3 %collective-permute-start.1 = (bf16[2,1024,256]{2,1,0:T(8,128)(2,1)}, bf16[2,1024,256]{2,1,0:T(8,128)(2,1)}, u32[]{:S(2)}, u32[]{:S(2)}) collective-permute-start(bf16[2,1024,256]{2,1,0:T(8,128)(2,1)} %refs_1_.7), channel_id=1, source_target_pairs={{0,16},{16,0},{32,48},{48,32},{64,80},{80,64},{96,112},{112,96},{1... | collective-permute-start | bytes 3145736 | tf_op jit(solution)/shard_map/ppermute | solution.py:45
  4.0 0.1 collective-permute-start.2
  4.1 1.9 %slice_bitcast_fusion.1 = bf16[1024,256]{1,0:T(8,128)(2,1)} fusion(bf16[2,1024,256]{2,1,0:T(8,128)(2,1)} %refs_1_.7), kind=kLoop, calls=%fused_computation.1 | loop fusion | bytes 1048576 | tf_op jit(solution)/shard_map/squeeze | solution.py:716
  5.9 0.0 collective-permute-start.3
  5.9 4.4 %local_grads.2 = (f32[3,2,128,256]{3,2,1,0:T(8,128)}, f32[3,2,2,256]{3,2,1,0:T(2,128)}, bf16[3,2,2,128,128]{4,3,2,1,0:T(8,128)(2,1)}) custom-call(bf16[2,1024,256]{2,1,0:T(8,128)(2,1)} %refs_1_.7, bf16[2,1024,256]{2,1,0:T(8,128)(2,1)} %refs_2_.7, f32[2,2,1024]{2,1,0:T(2,128)} %r_ref.3, f32[2]{0:T(128)} %refs_0_.3, f32[2,128,256]{2,1,0:T(8,128)} %refs_1_.4, ...), custom_call_target="tpu_custom_call" | custom-call | flops 805306368 | bytes 1048576 | tf_op jit(solution)/shard_map/local_grads/pallas_call | solution.py:126
  10.3 6.0 %all-to-all-start = ((bf16[16,96,128]{2,1,0:T(8,128)(2,1)}), bf16[16,96,128]{2,1,0:T(8,128)(2,1)S(1)}, u32[]{:S(2)}, u32[]{:S(2)}) async-start(bf16[16,96,128]{2,1,0:T(8,128)(2,1)} %bitcast.14), calls=%async_computation | async-start | bytes 786432 | tf_op jit(solution)/shard_map/all_to_all | solution.py:676
  16.3 1.9 %slice_bitcast_fusion.2 = bf16[1024,256]{1,0:T(8,128)(2,1)} fusion(bf16[2,1024,256]{2,1,0:T(8,128)(2,1)} %refs_0_.5), kind=kLoop, calls=%fused_computation.2 | loop fusion | bytes 1048576 | tf_op jit(solution)/shard_map/squeeze | solution.py:721
  18.1 3.5 %collective-permute-start = (bf16[1024,256]{1,0:T(8,128)(2,1)}, bf16[1024,256]{1,0:T(8,128)(2,1)S(1)}, u32[]{:S(2)}, u32[]{:S(2)}) collective-permute-start(bf16[1024,256]{1,0:T(8,128)(2,1)} %slice_bitcast_fusion.2), channel_id=1, source_target_pairs={{0,224},{16,240},{32,0},{48,16},{64,32},{80,48},{96,64},{112,80},{... | collective-permute-start | bytes 1572872 | tf_op jit(solution)/shard_map/ppermute | solution.py:45
  21.6 0.0 copy-done.1
  21.6 0.8 slice_bitcast_fusion
  22.5 0.0 collective-permute-done.3.refs_5_
  22.5 0.0 collective-permute-start.4
  22.5 3.6 %all-to-all-done.x_ref = bf16[16,96,128]{2,1,0:T(8,128)(2,1)S(1)} async-done(((bf16[16,96,128]{2,1,0:T(8,128)(2,1)}), bf16[16,96,128]{2,1,0:T(8,128)(2,1)S(1)}, u32[]{:S(2)}, u32[]{:S(2)}) %all-to-all-start) | async-done | bytes 393248 | tf_op jit(solution)/shard_map/all_to_all | solution.py:676
  26.1 0.8 add_parts.2
  26.9 4.0 %all-to-all-start.1 = ((bf16[16,96,128]{2,1,0:T(8,128)(2,1)}), bf16[16,96,128]{2,1,0:T(8,128)(2,1)S(1)}, u32[]{:S(2)}, u32[]{:S(2)}) async-start(bf16[16,96,128]{2,1,0:T(8,128)(2,1)} %add_parts.2), calls=%async_computation.1 | async-start | bytes 786432 | tf_op jit(solution)/shard_map/all_to_all | solution.py:676
  30.9 3.2 %collective-permute-done.refs_0_ = bf16[1024,256]{1,0:T(8,128)(2,1)S(1)} collective-permute-done((bf16[1024,256]{1,0:T(8,128)(2,1)}, bf16[1024,256]{1,0:T(8,128)(2,1)S(1)}, u32[]{:S(2)}, u32[]{:S(2)}) %collective-permute-start) | collective-permute-done | bytes 524320 | tf_op jit(solution)/shard_map/ppermute | solution.py:45
  34.2 1.5 %collective-permute-start.5 = (bf16[1024,256]{1,0:T(8,128)(2,1)}, bf16[1024,256]{1,0:T(8,128)(2,1)}, u32[]{:S(2)}, u32[]{:S(2)}) collective-permute-start(bf16[1024,256]{1,0:T(8,128)(2,1)} %collective-permute-done.3.refs_5_), channel_id=1, source_target_pairs={{0,16},{16,0},{32,48},{48,32},{64,80},{80,64},{96,112},{112,96},{1... | collective-permute-start | bytes 1572872 | tf_op jit(solution)/shard_map/ppermute | solution.py:45
  35.7 0.0 collective-permute-done.1.refs_3_
  35.7 0.0 collective-permute-done.2.refs_4_
  35.7 0.0 copy-done
  35.7 0.0 copy-start.6
  35.7 3.4 %remote_part.1 = (bf16[1024,256]{1,0:T(8,128)(2,1)}, f32[2,8,1024]{2,1,0:T(8,128)S(1)}) custom-call(s32[1]{0:T(128)} %bitcast.1.rank_ref, bf16[1024,256]{1,0:T(8,128)(2,1)S(1)} %collective-permute-done.refs_0_, bf16[2,1024,256]{2,1,0:T(8,128)(2,1)S(1)} %copy-done, bf16[2,1024,256]{2,1,0:T(8,128)(2,1)S(1)} %copy-done.1, ...), custom_call_target="tpu_custom_call" | custom-call | flops 2147483648 | bytes 3145728 | tf_op jit(solution)/shard_map/remote_part/pallas_call | solution.py:519
  39.1 3.6 %all-to-all-done.1 = bf16[16,96,128]{2,1,0:T(8,128)(2,1)S(1)} async-done(((bf16[16,96,128]{2,1,0:T(8,128)(2,1)}), bf16[16,96,128]{2,1,0:T(8,128)(2,1)S(1)}, u32[]{:S(2)}, u32[]{:S(2)}) %all-to-all-start.1) | async-done | bytes 393248 | tf_op jit(solution)/shard_map/all_to_all | solution.py:676
  42.7 0.1 collective-permute-start.8
  42.8 0.5 collective-permute-start.7
  43.3 0.0 collective-permute-done.4.refs_6_
  43.3 0.6 collective-permute-start.6
  43.9 0.0 copy-done.6
  43.9 1.1 copy-done.5
  45.0 4.8 %weight_step.2.refs_0_.refs_7_.w_hbm = f32[3,2,128,256]{3,2,1,0:T(8,128)S(1)} custom-call(bf16[3,2,2,128,128]{4,3,2,1,0:T(8,128)(2,1)S(1)} %bitcast.12, f32[3,2,128,256]{3,2,1,0:T(8,128)S(1)} %copy-done.5, f32[3,2,2,256]{3,2,1,0:T(2,128)S(1)} %copy-done.6), custom_call_target="tpu_custom_call" | custom-call | flops 5033164800 | bytes 1966080 | tf_op jit(solution)/shard_map/weight_step/pallas_call | solution.py:207
  49.9 0.0 copy-done.4
  49.9 0.0 copy-start.2
  49.9 2.7 %local_grads.3 = bf16[3,2,2,128,128]{4,3,2,1,0:T(8,128)(2,1)} custom-call(bf16[2,1024,256]{2,1,0:T(8,128)(2,1)S(1)} %copy-done, bf16[2,1024,256]{2,1,0:T(8,128)(2,1)S(1)} %copy-done.1, f32[2,2,1024]{2,1,0:T(2,128)S(1)} %copy-done.4, f32[3,2,128,256]{3,2,1,0:T(8,128)S(1)} %weight_step.2.refs_0_.refs_7_.w_hbm), custom_call_target="tpu_custom_call" | custom-call | flops 805306368 | bytes 1048576 | tf_op jit(solution)/shard_map/local_grads/pallas_call | solution.py:126
  52.7 17.3 %all-to-all-start.2 = ((bf16[16,96,128]{2,1,0:T(8,128)(2,1)}), bf16[16,96,128]{2,1,0:T(8,128)(2,1)S(1)}, u32[]{:S(2)}, u32[]{:S(2)}) async-start(bf16[16,96,128]{2,1,0:T(8,128)(2,1)} %bitcast.4), calls=%async_computation.2 | async-start | bytes 786432 | tf_op jit(solution)/shard_map/all_to_all | solution.py:676
  70.0 0.0 collective-permute-done.5.refs_7_
  70.0 0.0 collective-permute-done.6.refs_8_
  70.0 0.8 copy-done.7
  70.8 35.1 %mix.1._ = bf16[2,1024,256]{2,1,0:T(8,128)(2,1)} custom-call(s32[1]{0:T(128)} %bitcast.1.rank_ref, bf16[2,1024,256]{2,1,0:T(8,128)(2,1)} %refs_0_.5, bf16[2,1024,256]{2,1,0:T(8,128)(2,1)} %refs_1_.7, bf16[2,1024,256]{2,1,0:T(8,128)(2,1)} %refs_2_.7, bf16[2,1024,256]{2,1,0:T(8,128)(2,1)} %collective-permute-done.1.refs_3_, ...), custom_call_target="tpu_custom_call" | custom-call | flops 4294967296 | bytes 4194304 | tf_op jit(solution)/shard_map/mix/pallas_call | solution.py:366
  105.9 0.0 all-to-all-done.2.x_ref
  105.9 0.8 add_parts.3
  106.7 5.7 %all-to-all-start.3 = ((bf16[16,96,128]{2,1,0:T(8,128)(2,1)}), bf16[16,96,128]{2,1,0:T(8,128)(2,1)S(1)}, u32[]{:S(2)}, u32[]{:S(2)}) async-start(bf16[16,96,128]{2,1,0:T(8,128)(2,1)} %add_parts.3), calls=%async_computation.3 | async-start | bytes 786432 | tf_op jit(solution)/shard_map/all_to_all | solution.py:676
  112.5 0.0 collective-permute-done.8.refs_6_
  112.5 0.0 collective-permute-done.7.refs_5_
  112.5 0.6 copy-done.8
  113.1 24.2 %finish.1 = bf16[2,1024,256]{2,1,0:T(8,128)(2,1)} custom-call(bf16[2,1024,256]{2,1,0:T(8,128)(2,1)} %mix.1._, s32[1]{0:T(128)} %bitcast.1.rank_ref, bf16[2,1024,256]{2,1,0:T(8,128)(2,1)} %refs_0_.5, bf16[2,1024,256]{2,1,0:T(8,128)(2,1)} %refs_1_.7, bf16[2,1024,256]{2,1,0:T(8,128)(2,1)} %refs_2_.7, ...), custom_call_target="tpu_custom_call", output_to_operand_aliasing={{}: (0, {})} | custom-call | flops 3758096384 | bytes 4194304 | tf_op jit(solution)/shard_map/finish/pallas_call | solution.py:639
  137.3 0.0 all-to-all-done.3
  137.3 0.0 copy-done.3
  137.3 5.5 %weight_step.3 = f32[3,2,128,256]{3,2,1,0:T(8,128)} custom-call(bf16[3,2,2,128,128]{4,3,2,1,0:T(8,128)(2,1)S(1)} %bitcast.13, f32[3,2,128,256]{3,2,1,0:T(8,128)S(1)} %copy-done.3, f32[3,2,2,256]{3,2,1,0:T(2,128)S(1)} %copy-done.6), custom_call_target="tpu_custom_call" | custom-call | flops 5033164800 | bytes 1966080 | tf_op jit(solution)/shard_map/weight_step/pallas_call | solution.py:207
  (8 shorter events, 0.0 us)
Async XLA Ops:
  0.6 35.1 %collective-permute-start.1 = (bf16[2,1024,256]{2,1,0:T(8,128)(2,1)}, bf16[2,1024,256]{2,1,0:T(8,128)(2,1)}, u32[]{:S(2)}, u32[]{:S(2)}) collective-permute-start(bf16[2,1024,256]{2,1,0:T(8,128)(2,1)} %refs_1_.7), channel_id=1, source_target_pairs={{0,16},{16,0},{32,48},{48,32},{64,80},{80,64},{96,112},{112,96},{1... | collective-permute-start | bytes 3145736 | tf_op jit(solution)/shard_map/ppermute | solution.py:45
  4.0 31.7 %collective-permute-start.2 = (bf16[2,1024,256]{2,1,0:T(8,128)(2,1)}, bf16[2,1024,256]{2,1,0:T(8,128)(2,1)}, u32[]{:S(2)}, u32[]{:S(2)}) collective-permute-start(bf16[2,1024,256]{2,1,0:T(8,128)(2,1)} %refs_2_.7), channel_id=1, source_target_pairs={{0,16},{16,0},{32,48},{48,32},{64,80},{80,64},{96,112},{112,96},{1... | collective-permute-start | bytes 3145736 | tf_op jit(solution)/shard_map/ppermute | solution.py:45
  5.9 16.6 %collective-permute-start.3 = (bf16[1024,256]{1,0:T(8,128)(2,1)}, bf16[1024,256]{1,0:T(8,128)(2,1)}, u32[]{:S(2)}, u32[]{:S(2)}) collective-permute-start(bf16[1024,256]{1,0:T(8,128)(2,1)} %slice_bitcast_fusion.1), channel_id=1, source_target_pairs={{0,32},{16,48},{32,64},{48,80},{64,96},{80,112},{96,128},{112,144}... | collective-permute-start | bytes 1572872 | tf_op jit(solution)/shard_map/ppermute | solution.py:45
  10.3 11.3 %copy-start.1 = (bf16[2,1024,256]{2,1,0:T(8,128)(2,1)S(1)}, bf16[2,1024,256]{2,1,0:T(8,128)(2,1)}, u32[]{:S(2)}) copy-start(bf16[2,1024,256]{2,1,0:T(8,128)(2,1)} %refs_2_.7) | copy-start | bytes 3145732
  10.3 15.8 %all-to-all-start = ((bf16[16,96,128]{2,1,0:T(8,128)(2,1)}), bf16[16,96,128]{2,1,0:T(8,128)(2,1)S(1)}, u32[]{:S(2)}, u32[]{:S(2)}) async-start(bf16[16,96,128]{2,1,0:T(8,128)(2,1)} %bitcast.14), calls=%async_computation | async-start | bytes 786432 | tf_op jit(solution)/shard_map/all_to_all | solution.py:676
  18.1 16.0 %collective-permute-start = (bf16[1024,256]{1,0:T(8,128)(2,1)}, bf16[1024,256]{1,0:T(8,128)(2,1)S(1)}, u32[]{:S(2)}, u32[]{:S(2)}) collective-permute-start(bf16[1024,256]{1,0:T(8,128)(2,1)} %slice_bitcast_fusion.2), channel_id=1, source_target_pairs={{0,224},{16,240},{32,0},{48,16},{64,32},{80,48},{96,64},{112,80},{... | collective-permute-start | bytes 1572872 | tf_op jit(solution)/shard_map/ppermute | solution.py:45
  22.5 13.2 %copy-start = (bf16[2,1024,256]{2,1,0:T(8,128)(2,1)S(1)}, bf16[2,1024,256]{2,1,0:T(8,128)(2,1)}, u32[]{:S(2)}) copy-start(bf16[2,1024,256]{2,1,0:T(8,128)(2,1)} %refs_1_.7) | copy-start | bytes 3145732
  22.5 20.8 %collective-permute-start.4 = (bf16[1024,256]{1,0:T(8,128)(2,1)}, bf16[1024,256]{1,0:T(8,128)(2,1)}, u32[]{:S(2)}, u32[]{:S(2)}) collective-permute-start(bf16[1024,256]{1,0:T(8,128)(2,1)} %slice_bitcast_fusion), channel_id=1, source_target_pairs={{0,32},{16,48},{32,64},{48,80},{64,96},{80,112},{96,128},{112,144}... | collective-permute-start | bytes 1572872 | tf_op jit(solution)/shard_map/ppermute | solution.py:45
  26.9 15.7 %all-to-all-start.1 = ((bf16[16,96,128]{2,1,0:T(8,128)(2,1)}), bf16[16,96,128]{2,1,0:T(8,128)(2,1)S(1)}, u32[]{:S(2)}, u32[]{:S(2)}) async-start(bf16[16,96,128]{2,1,0:T(8,128)(2,1)} %add_parts.2), calls=%async_computation.1 | async-start | bytes 786432 | tf_op jit(solution)/shard_map/all_to_all | solution.py:676
  34.2 35.8 %collective-permute-start.5 = (bf16[1024,256]{1,0:T(8,128)(2,1)}, bf16[1024,256]{1,0:T(8,128)(2,1)}, u32[]{:S(2)}, u32[]{:S(2)}) collective-permute-start(bf16[1024,256]{1,0:T(8,128)(2,1)} %collective-permute-done.3.refs_5_), channel_id=1, source_target_pairs={{0,16},{16,0},{32,48},{48,32},{64,80},{80,64},{96,112},{112,96},{1... | collective-permute-start | bytes 1572872 | tf_op jit(solution)/shard_map/ppermute | solution.py:45
  35.7 8.2 %copy-start.6 = (f32[3,2,2,256]{3,2,1,0:T(2,128)S(1)}, f32[3,2,2,256]{3,2,1,0:T(2,128)}, u32[]{:S(2)}) copy-start(f32[3,2,2,256]{3,2,1,0:T(2,128)} %get-tuple-element.24.limits_hbm) | copy-start | bytes 36868
  42.7 69.8 %collective-permute-start.8 = (f32[2,8,1024]{2,1,0:T(8,128)S(1)}, f32[2,8,1024]{2,1,0:T(8,128)S(1)}, u32[]{:S(2)}, u32[]{:S(2)}) collective-permute-start(f32[2,8,1024]{2,1,0:T(8,128)S(1)} %get-tuple-element.29), channel_id=1, source_target_pairs={{0,32},{16,48},{32,64},{48,80},{64,96},{80,112},{96,128},{112,144}... | collective-permute-start | bytes 196616 | tf_op jit(solution)/shard_map/ppermute | solution.py:45
  42.8 69.7 %collective-permute-start.7 = (bf16[1024,256]{1,0:T(8,128)(2,1)}, bf16[1024,256]{1,0:T(8,128)(2,1)}, u32[]{:S(2)}, u32[]{:S(2)}) collective-permute-start(bf16[1024,256]{1,0:T(8,128)(2,1)} %get-tuple-element.28), channel_id=1, source_target_pairs={{0,32},{16,48},{32,64},{48,80},{64,96},{80,112},{96,128},{112,144}... | collective-permute-start | bytes 1572872 | tf_op jit(solution)/shard_map/ppermute | solution.py:45
  43.3 26.7 %collective-permute-start.6 = (bf16[1024,256]{1,0:T(8,128)(2,1)}, bf16[1024,256]{1,0:T(8,128)(2,1)S(1)}, u32[]{:S(2)}, u32[]{:S(2)}) collective-permute-start(bf16[1024,256]{1,0:T(8,128)(2,1)} %collective-permute-done.4.refs_6_), channel_id=1, source_target_pairs={{0,16},{16,0},{32,48},{48,32},{64,80},{80,64},{96,112},{112,96},{1... | collective-permute-start | bytes 1572872 | tf_op jit(solution)/shard_map/ppermute | solution.py:45
  43.9 1.1 copy-start.5
  45.0 4.9 %copy-start.4 = (f32[2,2,1024]{2,1,0:T(2,128)S(1)}, f32[2,2,1024]{2,1,0:T(2,128)}, u32[]{:S(2)}) copy-start(f32[2,2,1024]{2,1,0:T(2,128)} %r_ref.3) | copy-start | bytes 49156
  49.9 2.8 %copy-start.2 = (f32[3,2,128,256]{3,2,1,0:T(8,128)}, f32[3,2,128,256]{3,2,1,0:T(8,128)S(1)}, u32[]{:S(2)}) copy-start(f32[3,2,128,256]{3,2,1,0:T(8,128)S(1)} %weight_step.2.refs_0_.refs_7_.w_hbm) | copy-start | bytes 2359300
  52.7 53.2 %all-to-all-start.2 = ((bf16[16,96,128]{2,1,0:T(8,128)(2,1)}), bf16[16,96,128]{2,1,0:T(8,128)(2,1)S(1)}, u32[]{:S(2)}, u32[]{:S(2)}) async-start(bf16[16,96,128]{2,1,0:T(8,128)(2,1)} %bitcast.4), calls=%async_computation.2 | async-start | bytes 786432 | tf_op jit(solution)/shard_map/all_to_all | solution.py:676
  70.0 0.8 copy-start.7
  106.7 30.6 %all-to-all-start.3 = ((bf16[16,96,128]{2,1,0:T(8,128)(2,1)}), bf16[16,96,128]{2,1,0:T(8,128)(2,1)S(1)}, u32[]{:S(2)}, u32[]{:S(2)}) async-start(bf16[16,96,128]{2,1,0:T(8,128)(2,1)} %add_parts.3), calls=%async_computation.3 | async-start | bytes 786432 | tf_op jit(solution)/shard_map/all_to_all | solution.py:676
  112.4 24.9 %copy-start.3 = (f32[3,2,128,256]{3,2,1,0:T(8,128)S(1)}, f32[3,2,128,256]{3,2,1,0:T(8,128)}, u32[]{:S(2)}) copy-start(f32[3,2,128,256]{3,2,1,0:T(8,128)} %copy-done.2) | copy-start | bytes 2359300
  112.5 0.6 copy-start.8
where the time goes:
time: 146 us; the launch traced here: 143 us
  Pallas kernels  81.8 us (56%)
  starting transfers between devices  42.7 us (29%)
  waiting for transfers between devices  10.5 us (7%)
  local copies, waits for them, and re-layouts  7.1 us (5%)
    pallas_call x1, Pallas kernels, mix(): pl.pallas_call(functools.partial(mix_kernel, group), out_shape=jax.ShapeD...  35.1 us
    all_to_all x4, starting transfers between devices, exchange(): return lax.all_to_all(tiles, 'seq', 0, 0, tiled=True)  33 us
    pallas_call x1, Pallas kernels, finish(): pl.pallas_call(functools.partial(finish_kernel, group), out_shape=jax.Sha...  24.2 us
    pallas_call x2, Pallas kernels, step(): pl.pallas_call(step_kernel, out_shape=jax.ShapeDtypeStruct(weights.shape,...  10.4 us
    ppermute x9, starting transfers between devices, move(): lax.ppermute(block, 'seq', [(i, route(i)) for i in range(lax.axis_size('s...  9.68 us
    all_to_all x4, waiting for transfers between devices, exchange(): return lax.all_to_all(tiles, 'seq', 0, 0, tiled=True)  7.24 us
    pallas_call x2, Pallas kernels, local_grads(): pl.pallas_call(functools.partial(grads_kernel, group), out_shape=out_shap...  7.12 us
    pallas_call x1, Pallas kernels, remote_part(): pl.pallas_call(functools.partial(remote_kernel, group, size), out_shape=[...  3.36 us
  transfers between devices with their start and end apart: 13, of which 3 were waited for; matrix products, arithmetic and copies ran while one was open for 3% of the time, Pallas kernels for 53%

commit v1 on v0

--- a/solution.py
+++ b/solution.py
@@ -718,7 +718,7 @@
         0, key_vectors, value_vectors, token_rates, first, step_sizes
     )
     far_values = send(after(value_vectors[0], (far_keys, partial)), 2)
-    asked = send(after(query_vectors[1], partial), -2)
+    asked = send(query_vectors[1], -2)
     early = [swap(t) for t in own[1:]]
     added = add_parts(exchange(partial.reshape(size, -1, HD)))
     summed = exchange(added)

time: 146 us -> 151 us (1.034)
  the two profiles are of different devices: /device:TPU:1 before, /device:TPU:103 now
where the time goes in v1:
time: 151 us
  Pallas kernels  81.9 us (54%)
  starting transfers between devices  39.2 us (26%)
  waiting for transfers between devices  22.2 us (15%)
  local copies, waits for them, and re-layouts  6.09 us (4%)
    pallas_call x1, Pallas kernels, mix(): pl.pallas_call(functools.partial(mix_kernel, group), out_shape=jax.ShapeD...  35.1 us
    pallas_call x1, Pallas kernels, finish(): pl.pallas_call(functools.partial(finish_kernel, group), out_shape=jax.Sha...  24.2 us
    all_to_all x4, waiting for transfers between devices, exchange(): return lax.all_to_all(tiles, 'seq', 0, 0, tiled=True)  21.2 us
    ppermute x9, starting transfers between devices, move(): lax.ppermute(block, 'seq', [(i, route(i)) for i in range(lax.axis_size('s...  21 us
    all_to_all x4, starting transfers between devices, exchange(): return lax.all_to_all(tiles, 'seq', 0, 0, tiled=True)  18.3 us
    pallas_call x2, Pallas kernels, step(): pl.pallas_call(step_kernel, out_shape=jax.ShapeDtypeStruct(weights.shape,...  10.4 us
    pallas_call x2, Pallas kernels, local_grads(): pl.pallas_call(functools.partial(grads_kernel, group), out_shape=out_shap...  7.24 us
    pallas_call x1, Pallas kernels, remote_part(): pl.pallas_call(functools.partial(remote_kernel, group, size), out_shape=[...  3.36 us
  transfers between devices with their start and end apart: 13, of which 3 were waited for; matrix products, arithmetic and copies ran while one was open for 2% of the time, Pallas kernels for 51%

profile of v1, /device:TPU:103, one launch (start us, length us, event | category | flops | bytes accessed | tf_op | source)
XLA Modules:
  0.0 150.5 jit_solution(3372027318816237979)
XLA Ops:
  0.6 0.0 copy-start.8
  0.6 0.8 collective-permute-start.1
  1.4 0.1 collective-permute-start.2
  1.5 1.9 %slice_bitcast_fusion.1 = bf16[1024,256]{1,0:T(8,128)(2,1)} fusion(bf16[2,1024,256]{2,1,0:T(8,128)(2,1)} %refs_1_.7), kind=kLoop, calls=%fused_computation.1 | loop fusion | bytes 1048576 | tf_op jit(solution)/shard_map/squeeze | solution.py:716
  3.4 1.3 collective-permute-start.3
  4.7 0.0 copy-done.8
  4.7 0.8 slice_bitcast_fusion.2
  5.5 2.3 %collective-permute-start = (bf16[1024,256]{1,0:T(8,128)(2,1)}, bf16[1024,256]{1,0:T(8,128)(2,1)S(1)}, u32[]{:S(2)}, u32[]{:S(2)}) collective-permute-start(bf16[1024,256]{1,0:T(8,128)(2,1)} %slice_bitcast_fusion.2), channel_id=1, source_target_pairs={{0,224},{16,240},{32,0},{48,16},{64,32},{80,48},{96,64},{112,80},{... | collective-permute-start | bytes 1572872 | tf_op jit(solution)/shard_map/ppermute | solution.py:45
  7.8 4.5 %local_grads.2 = (f32[3,2,128,256]{3,2,1,0:T(8,128)}, f32[3,2,2,256]{3,2,1,0:T(2,128)}, bf16[3,2,2,128,128]{4,3,2,1,0:T(8,128)(2,1)}) custom-call(bf16[2,1024,256]{2,1,0:T(8,128)(2,1)} %refs_1_.7, bf16[2,1024,256]{2,1,0:T(8,128)(2,1)} %refs_2_.7, f32[2,2,1024]{2,1,0:T(2,128)} %r_ref.3, f32[2]{0:T(128)} %refs_0_.3, f32[2,128,256]{2,1,0:T(8,128)} %refs_1_.4, ...), custom_call_target="tpu_custom_call" | custom-call | flops 805306368 | bytes 1048576 | tf_op jit(solution)/shard_map/local_grads/pallas_call | solution.py:126
  12.2 4.8 %all-to-all-start = ((bf16[16,96,128]{2,1,0:T(8,128)(2,1)}), bf16[16,96,128]{2,1,0:T(8,128)(2,1)S(1)}, u32[]{:S(2)}, u32[]{:S(2)}) async-start(bf16[16,96,128]{2,1,0:T(8,128)(2,1)} %bitcast.14), calls=%async_computation | async-start | bytes 786432 | tf_op jit(solution)/shard_map/all_to_all | solution.py:676
  17.1 0.0 copy-done.1
  17.1 0.0 copy-start.2
  17.1 0.8 slice_bitcast_fusion
  17.9 1.0 collective-permute-done.3.refs_5_
  18.9 0.2 collective-permute-start.4
  19.1 17.3 %all-to-all-done.x_ref = bf16[16,96,128]{2,1,0:T(8,128)(2,1)S(1)} async-done(((bf16[16,96,128]{2,1,0:T(8,128)(2,1)}), bf16[16,96,128]{2,1,0:T(8,128)(2,1)S(1)}, u32[]{:S(2)}, u32[]{:S(2)}) %all-to-all-start) | async-done | bytes 393248 | tf_op jit(solution)/shard_map/all_to_all | solution.py:676
  36.4 0.8 add_parts.2
  37.2 3.5 %all-to-all-start.1 = ((bf16[16,96,128]{2,1,0:T(8,128)(2,1)}), bf16[16,96,128]{2,1,0:T(8,128)(2,1)S(1)}, u32[]{:S(2)}, u32[]{:S(2)}) async-start(bf16[16,96,128]{2,1,0:T(8,128)(2,1)} %add_parts.2), calls=%async_computation.1 | async-start | bytes 786432 | tf_op jit(solution)/shard_map/all_to_all | solution.py:676
  40.7 0.0 collective-permute-done.refs_0_
  40.7 0.1 collective-permute-start.5
  40.8 0.0 collective-permute-done.1.refs_3_
  40.8 0.0 collective-permute-done.2.refs_4_
  40.8 0.0 copy-done.2
  40.9 0.0 copy-done
  40.9 3.4 %remote_part.1 = (bf16[1024,256]{1,0:T(8,128)(2,1)}, f32[2,8,1024]{2,1,0:T(8,128)S(1)}) custom-call(s32[1]{0:T(128)} %bitcast.1.rank_ref, bf16[1024,256]{1,0:T(8,128)(2,1)S(1)} %collective-permute-done.refs_0_, bf16[2,1024,256]{2,1,0:T(8,128)(2,1)S(1)} %copy-done, bf16[2,1024,256]{2,1,0:T(8,128)(2,1)S(1)} %copy-done.2, ...), custom_call_target="tpu_custom_call" | custom-call | flops 2147483648 | bytes 3145728 | tf_op jit(solution)/shard_map/remote_part/pallas_call | solution.py:519
  44.2 3.9 %all-to-all-done.1 = bf16[16,96,128]{2,1,0:T(8,128)(2,1)S(1)} async-done(((bf16[16,96,128]{2,1,0:T(8,128)(2,1)}), bf16[16,96,128]{2,1,0:T(8,128)(2,1)S(1)}, u32[]{:S(2)}, u32[]{:S(2)}) %all-to-all-start.1) | async-done | bytes 393248 | tf_op jit(solution)/shard_map/all_to_all | solution.py:676
  48.2 0.2 collective-permute-start.8
  48.4 0.8 collective-permute-start.7
  49.2 0.0 collective-permute-done.4.refs_6_
  49.2 15.2 %collective-permute-start.6 = (bf16[1024,256]{1,0:T(8,128)(2,1)}, bf16[1024,256]{1,0:T(8,128)(2,1)S(1)}, u32[]{:S(2)}, u32[]{:S(2)}) collective-permute-start(bf16[1024,256]{1,0:T(8,128)(2,1)} %collective-permute-done.4.refs_6_), channel_id=1, source_target_pairs={{0,16},{16,0},{32,48},{48,32},{64,80},{80,64},{96,112},{112,96},{1... | collective-permute-start | bytes 1572872 | tf_op jit(solution)/shard_map/ppermute | solution.py:45
  64.4 0.0 copy-done.7
  64.4 1.1 copy-done.6
  65.5 4.8 %weight_step.2.refs_0_.refs_7_.w_hbm = f32[3,2,128,256]{3,2,1,0:T(8,128)S(1)} custom-call(bf16[3,2,2,128,128]{4,3,2,1,0:T(8,128)(2,1)S(1)} %bitcast.12, f32[3,2,128,256]{3,2,1,0:T(8,128)S(1)} %copy-done.6, f32[3,2,2,256]{3,2,1,0:T(2,128)S(1)} %copy-done.7), custom_call_target="tpu_custom_call" | custom-call | flops 5033164800 | bytes 1966080 | tf_op jit(solution)/shard_map/weight_step/pallas_call | solution.py:207
  70.4 2.8 %local_grads.3 = bf16[3,2,2,128,128]{4,3,2,1,0:T(8,128)(2,1)} custom-call(bf16[2,1024,256]{2,1,0:T(8,128)(2,1)S(1)} %copy-done, bf16[2,1024,256]{2,1,0:T(8,128)(2,1)S(1)} %copy-done.2, f32[2,2,1024]{2,1,0:T(2,128)S(1)} %copy-done.5, f32[3,2,128,256]{3,2,1,0:T(8,128)S(1)} %weight_step.2.refs_0_.refs_7_.w_hbm), custom_call_target="tpu_custom_call" | custom-call | flops 805306368 | bytes 1048576 | tf_op jit(solution)/shard_map/local_grads/pallas_call | solution.py:126
  73.2 4.3 %all-to-all-start.2 = ((bf16[16,96,128]{2,1,0:T(8,128)(2,1)}), bf16[16,96,128]{2,1,0:T(8,128)(2,1)S(1)}, u32[]{:S(2)}, u32[]{:S(2)}) async-start(bf16[16,96,128]{2,1,0:T(8,128)(2,1)} %bitcast.4), calls=%async_computation.2 | async-start | bytes 786432 | tf_op jit(solution)/shard_map/all_to_all | solution.py:676
  77.4 0.0 collective-permute-done.5.refs_7_
  77.4 0.0 collective-permute-done.6.refs_8_
  77.5 0.8 copy-done.9
  78.3 35.1 %mix.1._ = bf16[2,1024,256]{2,1,0:T(8,128)(2,1)} custom-call(s32[1]{0:T(128)} %bitcast.1.rank_ref, bf16[2,1024,256]{2,1,0:T(8,128)(2,1)} %refs_0_.5, bf16[2,1024,256]{2,1,0:T(8,128)(2,1)} %refs_1_.7, bf16[2,1024,256]{2,1,0:T(8,128)(2,1)} %refs_2_.7, bf16[2,1024,256]{2,1,0:T(8,128)(2,1)} %collective-permute-done.1.refs_3_, ...), custom_call_target="tpu_custom_call" | custom-call | flops 4294967296 | bytes 4194304 | tf_op jit(solution)/shard_map/mix/pallas_call | solution.py:366
  113.4 0.0 all-to-all-done.2.x_ref
  113.4 0.8 add_parts.3
  114.2 5.7 %all-to-all-start.3 = ((bf16[16,96,128]{2,1,0:T(8,128)(2,1)}), bf16[16,96,128]{2,1,0:T(8,128)(2,1)S(1)}, u32[]{:S(2)}, u32[]{:S(2)}) async-start(bf16[16,96,128]{2,1,0:T(8,128)(2,1)} %add_parts.3), calls=%async_computation.3 | async-start | bytes 786432 | tf_op jit(solution)/shard_map/all_to_all | solution.py:676
  119.9 0.0 collective-permute-done.8.refs_6_
  119.9 0.0 collective-permute-done.7.refs_5_
  120.0 0.6 copy-done.10
  120.6 24.2 %finish.1 = bf16[2,1024,256]{2,1,0:T(8,128)(2,1)} custom-call(bf16[2,1024,256]{2,1,0:T(8,128)(2,1)} %mix.1._, s32[1]{0:T(128)} %bitcast.1.rank_ref, bf16[2,1024,256]{2,1,0:T(8,128)(2,1)} %refs_0_.5, bf16[2,1024,256]{2,1,0:T(8,128)(2,1)} %refs_1_.7, bf16[2,1024,256]{2,1,0:T(8,128)(2,1)} %refs_2_.7, ...), custom_call_target="tpu_custom_call", output_to_operand_aliasing={{}: (0, {})} | custom-call | flops 3758096384 | bytes 4194304 | tf_op jit(solution)/shard_map/finish/pallas_call | solution.py:639
  144.8 0.0 all-to-all-done.3
  144.8 5.5 %weight_step.3 = f32[3,2,128,256]{3,2,1,0:T(8,128)} custom-call(bf16[3,2,2,128,128]{4,3,2,1,0:T(8,128)(2,1)S(1)} %bitcast.13, f32[3,2,128,256]{3,2,1,0:T(8,128)S(1)} %copy-done.4, f32[3,2,2,256]{3,2,1,0:T(2,128)S(1)} %copy-done.7), custom_call_target="tpu_custom_call" | custom-call | flops 5033164800 | bytes 1966080 | tf_op jit(solution)/shard_map/weight_step/pallas_call | solution.py:207
  (12 shorter events, 0.0 us)
Async XLA Ops:
  0.6 4.0 %copy-start.8 = (bf16[2,1024,256]{2,1,0:T(8,128)(2,1)S(1)}, bf16[2,1024,256]{2,1,0:T(8,128)(2,1)}, u32[]{:S(2)}) copy-start(bf16[2,1024,256]{2,1,0:T(8,128)(2,1)} %refs_0_.5) | copy-start | bytes 3145732
  0.6 40.2 %collective-permute-start.1 = (bf16[2,1024,256]{2,1,0:T(8,128)(2,1)}, bf16[2,1024,256]{2,1,0:T(8,128)(2,1)}, u32[]{:S(2)}, u32[]{:S(2)}) collective-permute-start(bf16[2,1024,256]{2,1,0:T(8,128)(2,1)} %refs_1_.7), channel_id=1, source_target_pairs={{0,16},{16,0},{32,48},{48,32},{64,80},{80,64},{96,112},{112,96},{1... | collective-permute-start | bytes 3145736 | tf_op jit(solution)/shard_map/ppermute | solution.py:45
  1.4 39.4 %collective-permute-start.2 = (bf16[2,1024,256]{2,1,0:T(8,128)(2,1)}, bf16[2,1024,256]{2,1,0:T(8,128)(2,1)}, u32[]{:S(2)}, u32[]{:S(2)}) collective-permute-start(bf16[2,1024,256]{2,1,0:T(8,128)(2,1)} %refs_2_.7), channel_id=1, source_target_pairs={{0,16},{16,0},{32,48},{48,32},{64,80},{80,64},{96,112},{112,96},{1... | collective-permute-start | bytes 3145736 | tf_op jit(solution)/shard_map/ppermute | solution.py:45
  3.4 15.5 %collective-permute-start.3 = (bf16[1024,256]{1,0:T(8,128)(2,1)}, bf16[1024,256]{1,0:T(8,128)(2,1)}, u32[]{:S(2)}, u32[]{:S(2)}) collective-permute-start(bf16[1024,256]{1,0:T(8,128)(2,1)} %slice_bitcast_fusion.1), channel_id=1, source_target_pairs={{0,32},{16,48},{32,64},{48,80},{64,96},{80,112},{96,128},{112,144}... | collective-permute-start | bytes 1572872 | tf_op jit(solution)/shard_map/ppermute | solution.py:45
  5.5 35.2 %collective-permute-start = (bf16[1024,256]{1,0:T(8,128)(2,1)}, bf16[1024,256]{1,0:T(8,128)(2,1)S(1)}, u32[]{:S(2)}, u32[]{:S(2)}) collective-permute-start(bf16[1024,256]{1,0:T(8,128)(2,1)} %slice_bitcast_fusion.2), channel_id=1, source_target_pairs={{0,224},{16,240},{32,0},{48,16},{64,32},{80,48},{96,64},{112,80},{... | collective-permute-start | bytes 1572872 | tf_op jit(solution)/shard_map/ppermute | solution.py:45
  7.8 9.3 %copy-start.1 = (bf16[2,1024,256]{2,1,0:T(8,128)(2,1)S(1)}, bf16[2,1024,256]{2,1,0:T(8,128)(2,1)}, u32[]{:S(2)}) copy-start(bf16[2,1024,256]{2,1,0:T(8,128)(2,1)} %refs_2_.7) | copy-start | bytes 3145732
  12.2 24.2 %all-to-all-start = ((bf16[16,96,128]{2,1,0:T(8,128)(2,1)}), bf16[16,96,128]{2,1,0:T(8,128)(2,1)S(1)}, u32[]{:S(2)}, u32[]{:S(2)}) async-start(bf16[16,96,128]{2,1,0:T(8,128)(2,1)} %bitcast.14), calls=%async_computation | async-start | bytes 786432 | tf_op jit(solution)/shard_map/all_to_all | solution.py:676
  17.1 23.8 %copy-start.2 = (bf16[2,1024,256]{2,1,0:T(8,128)(2,1)S(1)}, bf16[2,1024,256]{2,1,0:T(8,128)(2,1)}, u32[]{:S(2)}) copy-start(bf16[2,1024,256]{2,1,0:T(8,128)(2,1)} %refs_2_.7) | copy-start | bytes 3145732
  17.9 22.9 %copy-start = (bf16[2,1024,256]{2,1,0:T(8,128)(2,1)S(1)}, bf16[2,1024,256]{2,1,0:T(8,128)(2,1)}, u32[]{:S(2)}) copy-start(bf16[2,1024,256]{2,1,0:T(8,128)(2,1)} %refs_1_.7) | copy-start | bytes 3145732
  18.9 30.3 %collective-permute-start.4 = (bf16[1024,256]{1,0:T(8,128)(2,1)}, bf16[1024,256]{1,0:T(8,128)(2,1)}, u32[]{:S(2)}, u32[]{:S(2)}) collective-permute-start(bf16[1024,256]{1,0:T(8,128)(2,1)} %slice_bitcast_fusion), channel_id=1, source_target_pairs={{0,32},{16,48},{32,64},{48,80},{64,96},{80,112},{96,128},{112,144}... | collective-permute-start | bytes 1572872 | tf_op jit(solution)/shard_map/ppermute | solution.py:45
  37.2 10.9 %all-to-all-start.1 = ((bf16[16,96,128]{2,1,0:T(8,128)(2,1)}), bf16[16,96,128]{2,1,0:T(8,128)(2,1)S(1)}, u32[]{:S(2)}, u32[]{:S(2)}) async-start(bf16[16,96,128]{2,1,0:T(8,128)(2,1)} %add_parts.2), calls=%async_computation.1 | async-start | bytes 786432 | tf_op jit(solution)/shard_map/all_to_all | solution.py:676
  40.7 36.7 %collective-permute-start.5 = (bf16[1024,256]{1,0:T(8,128)(2,1)}, bf16[1024,256]{1,0:T(8,128)(2,1)}, u32[]{:S(2)}, u32[]{:S(2)}) collective-permute-start(bf16[1024,256]{1,0:T(8,128)(2,1)} %collective-permute-done.3.refs_5_), channel_id=1, source_target_pairs={{0,16},{16,0},{32,48},{48,32},{64,80},{80,64},{96,112},{112,96},{1... | collective-permute-start | bytes 1572872 | tf_op jit(solution)/shard_map/ppermute | solution.py:45
  40.9 23.5 %copy-start.7 = (f32[3,2,2,256]{3,2,1,0:T(2,128)S(1)}, f32[3,2,2,256]{3,2,1,0:T(2,128)}, u32[]{:S(2)}) copy-start(f32[3,2,2,256]{3,2,1,0:T(2,128)} %get-tuple-element.22.limits_hbm) | copy-start | bytes 36868
  48.2 71.8 %collective-permute-start.8 = (f32[2,8,1024]{2,1,0:T(8,128)S(1)}, f32[2,8,1024]{2,1,0:T(8,128)S(1)}, u32[]{:S(2)}, u32[]{:S(2)}) collective-permute-start(f32[2,8,1024]{2,1,0:T(8,128)S(1)} %get-tuple-element.27), channel_id=1, source_target_pairs={{0,32},{16,48},{32,64},{48,80},{64,96},{80,112},{96,128},{112,144}... | collective-permute-start | bytes 196616 | tf_op jit(solution)/shard_map/ppermute | solution.py:45
  48.4 71.6 %collective-permute-start.7 = (bf16[1024,256]{1,0:T(8,128)(2,1)}, bf16[1024,256]{1,0:T(8,128)(2,1)}, u32[]{:S(2)}, u32[]{:S(2)}) collective-permute-start(bf16[1024,256]{1,0:T(8,128)(2,1)} %get-tuple-element.26), channel_id=1, source_target_pairs={{0,32},{16,48},{32,64},{48,80},{64,96},{80,112},{96,128},{112,144}... | collective-permute-start | bytes 1572872 | tf_op jit(solution)/shard_map/ppermute | solution.py:45
  49.2 28.3 %collective-permute-start.6 = (bf16[1024,256]{1,0:T(8,128)(2,1)}, bf16[1024,256]{1,0:T(8,128)(2,1)S(1)}, u32[]{:S(2)}, u32[]{:S(2)}) collective-permute-start(bf16[1024,256]{1,0:T(8,128)(2,1)} %collective-permute-done.4.refs_6_), channel_id=1, source_target_pairs={{0,16},{16,0},{32,48},{48,32},{64,80},{80,64},{96,112},{112,96},{1... | collective-permute-start | bytes 1572872 | tf_op jit(solution)/shard_map/ppermute | solution.py:45
  64.4 1.1 copy-start.6
  65.5 4.8 %copy-start.5 = (f32[2,2,1024]{2,1,0:T(2,128)S(1)}, f32[2,2,1024]{2,1,0:T(2,128)}, u32[]{:S(2)}) copy-start(f32[2,2,1024]{2,1,0:T(2,128)} %r_ref.3) | copy-start | bytes 49156
  70.4 2.8 %copy-start.3 = (f32[3,2,128,256]{3,2,1,0:T(8,128)}, f32[3,2,128,256]{3,2,1,0:T(8,128)S(1)}, u32[]{:S(2)}) copy-start(f32[3,2,128,256]{3,2,1,0:T(8,128)S(1)} %weight_step.2.refs_0_.refs_7_.w_hbm) | copy-start | bytes 2359300
  73.2 40.2 %all-to-all-start.2 = ((bf16[16,96,128]{2,1,0:T(8,128)(2,1)}), bf16[16,96,128]{2,1,0:T(8,128)(2,1)S(1)}, u32[]{:S(2)}, u32[]{:S(2)}) async-start(bf16[16,96,128]{2,1,0:T(8,128)(2,1)} %bitcast.4), calls=%async_computation.2 | async-start | bytes 786432 | tf_op jit(solution)/shard_map/all_to_all | solution.py:676
  77.5 0.8 copy-start.9
  114.2 30.6 %all-to-all-start.3 = ((bf16[16,96,128]{2,1,0:T(8,128)(2,1)}), bf16[16,96,128]{2,1,0:T(8,128)(2,1)S(1)}, u32[]{:S(2)}, u32[]{:S(2)}) async-start(bf16[16,96,128]{2,1,0:T(8,128)(2,1)} %add_parts.3), calls=%async_computation.3 | async-start | bytes 786432 | tf_op jit(solution)/shard_map/all_to_all | solution.py:676
  119.9 24.9 %copy-start.4 = (f32[3,2,128,256]{3,2,1,0:T(8,128)S(1)}, f32[3,2,128,256]{3,2,1,0:T(8,128)}, u32[]{:S(2)}) copy-start(f32[3,2,128,256]{3,2,1,0:T(8,128)} %copy-done.3) | copy-start | bytes 2359300
  119.9 0.6 copy-start.10
